TPU v7x, 32 devices: a whole 2x2x4 slice. The times are simulated.
32 devices in a mesh: rows: 32 (over z, y, x, core), rep: 1.
Axes of the slice: x: 2, y: 2, z: 4, core: 2. Of those that a mesh axis runs over, the one named last changes fastest.
Arguments:
- features: bfloat16 [32768, 128], P(('rows', 'rep')), may hold values from -6 to 6
- weight: bfloat16 [128, 256], replicated, may hold values from -0.5 to 0.5
- shift_bias: float32 [256], replicated, may hold values from -3 to 3
- norm_gain: float32 [256], replicated, may hold values from 0.25 to 1.75
- tile_values: bfloat16 [256, 1, 88, 128, 128], P('rows', 'rep'), as said below
- tile_cols: int32 [256, 1, 88], P('rows', 'rep'), may hold values from 0 to 255, all different within a row
- tile_counts: int32 [256, 1], P('rows', 'rep'), may hold values from 1 to 88, as said below
- block_order: int32 [1, 256], replicated, may hold values from 0 to 255, each once within a row
Outputs:
- node_out: bfloat16 [32768, 256], P(('rows', 'rep'))
Inputs may be any that keep to these rules, and one draw needn't show every extreme that they name: Slots 0 to tile_counts - 1 of a row block and column set are live, the rest are ignored; the largest count is reached. `tile_values`: tile entries are nonnegative.
All inputs are finite; a program needn't handle non-finite values.
Results may differ from a plain program's by a relative error of at most 0.0052.
Values may be sent and summed in bfloat16 or wider, within the bound.
A program may use at most 192 MiB of HBM per device.

v0:
```python
import jax
import jax.numpy as jnp
from jax import lax
from jax.sharding import PartitionSpec as P


def per_device(
    features, weight, shift_bias, norm_gain, tile_values, tile_cols, tile_counts, block_order
):
    row_blocks = tile_values.shape[0]
    slot_count = tile_values.shape[2]
    block_size = tile_values.shape[3]
    hidden_width = weight.shape[1]
    gathered = lax.all_gather(features, "rows", axis=0, tiled=True)
    panel_rows = jnp.dot(gathered, weight, preferred_element_type=jnp.float32).astype(jnp.bfloat16)
    set_blocks = panel_rows.shape[0] // block_size
    panel_blocks = panel_rows.reshape(set_blocks, block_size, hidden_width)
    order_mine = lax.dynamic_index_in_dim(block_order, lax.axis_index("rep"), 0, keepdims=False)
    column_ids = tile_cols.reshape(row_blocks, slot_count)
    matches = column_ids[:, :, None] == jnp.arange(set_blocks, dtype=jnp.int32)[None, None, :]
    positions = jnp.sum(jnp.where(matches, order_mine[None, None, :], 0), axis=2)
    tile_block = tile_values.reshape(row_blocks, slot_count, block_size, block_size)
    live_count = tile_counts.reshape(row_blocks)
    picked_rows = panel_blocks[positions]
    live_mask = jnp.arange(slot_count, dtype=jnp.int32)[None, :] < live_count[:, None]
    picked_rows = jnp.where(live_mask[:, :, None, None], picked_rows, jnp.zeros((), jnp.bfloat16))
    summed = jnp.einsum(
        "bkij,bkjh->bih", tile_block, picked_rows, preferred_element_type=jnp.float32
    )
    row_half = lax.psum_scatter(
        summed.reshape(row_blocks * block_size, hidden_width),
        "rep",
        scatter_dimension=0,
        tiled=True,
    )
    hidden = jnp.maximum(row_half + shift_bias, 0.0)
    row_mean = jnp.mean(hidden, axis=1, keepdims=True)
    centered = hidden - row_mean
    row_var = jnp.mean(centered * centered, axis=1, keepdims=True)
    return (centered / jnp.sqrt(row_var + 1e-05) * norm_gain).astype(jnp.bfloat16)


def solution(mesh):
    in_specs = (
        P(("rows", "rep"), None),
        P(),
        P(),
        P(),
        P("rows", "rep", None, None, None),
        P("rows", "rep", None),
        P("rows", "rep"),
        P(),
    )
    out_specs = P(("rows", "rep"), None)
    return jax.shard_map(
        per_device, mesh=mesh, in_specs=in_specs, out_specs=out_specs, check_vma=False
    )
```

profile of v0, /device:TPU:0, one launch (start us, length us, event | category | flops | bytes accessed | tf_op | source)
XLA Modules:
  0.0 162.1 jit_solution(13353589503720990027)
XLA Ops:
  6.5 0.0 copy-start
  6.5 0.0 all-gather.2.cloned.1.call-start
  6.5 0.7 all-gather.2.cloned.1.call-update
  7.3 1.0 select_reduce_fusion
  8.3 0.1 reshape.94
  8.4 0.7 iota_compare_fusion.1
  9.1 81.3 %all-gather.2.cloned.1.call-done = bf16[32768,128]{1,0:T(8,128)(2,1)} async-done(((bf16[1024,128]{1,0:T(8,128)(2,1)}), bf16[32768,128]{1,0:T(8,128)(2,1)}) %all-gather.2.cloned.1.call-update) | async-done | bytes 8388624 | tf_op jit(solution)/shard_map/all_gather | solution.py:14
  90.4 0.0 copy-done
  90.4 13.6 %convolution_convert_fusion = bf16[32768,256]{1,0:T(8,128)(2,1)} fusion(bf16[32768,128]{1,0:T(8,128)(2,1)} %all-gather.2.cloned.1.call-done, bf16[128,256]{1,0:T(8,128)(2,1)S(1)} %copy-done), kind=kOutput, calls=%fused_computation.4 | convolution fusion | flops 2155872256 | bytes 25231360 | tf_op jit(solution)/shard_map/dot_general | solution.py:15
  104.0 0.0 copy-start.2
  104.0 26.7 %gather_fusion = bf16[704,128,256]{2,1,0:T(8,128)(2,1)} fusion(bf16[256,128,256]{2,1,0:T(8,128)(2,1)} %bitcast.44, s32[1024]{0:T(1024)S(1)} %pad_clamp_fusion), kind=kCustom, calls=%fused_computation | custom fusion | bytes 92277504 | tf_op jit(solution)/shard_map/gather | solution.py:24
  130.8 0.0 copy-done.2
  130.8 0.0 copy-start.3
  130.8 0.0 copy-start.1
  130.8 22.8 %fusion.11 = (f32[8,128]{1,0:T(8,128)S(1)}, f32[8,256,128,1]{1,2,3,0:T(8,128)S(1)}) fusion(f32[256]{0:T(256)S(1)} %copy-done.2, bf16[8,88,128,256]{3,2,1,0:T(8,128)(2,1)} %bitcast.45, pred[8,88]{1,0:T(8,128)(4,1)S(1)} %iota_compare_fusion.1, bf16[8,1,88,128,128]{4,3,2,1,0:T(8,128)(2,1)} %param.12), kind=kOutput, calls=%fused_computation.16 | convolution fusion | flops 5929434112 | bytes 70260416 | tf_op jit(solution)/shard_map/bkij,bkjh->bih/dot_general | solution.py:27
  153.7 0.4 multiply_reduce_fusion
  154.1 0.0 copy-done.3
  154.1 1.1 fusion.10
  155.2 0.0 copy-done.1
  (4 shorter events, 0.0 us)
Async XLA Ops:
  6.5 83.9 %copy-start = (bf16[128,256]{1,0:T(8,128)(2,1)S(1)}, bf16[128,256]{1,0:T(8,128)(2,1)}, u32[]{:S(2)}) copy-start(bf16[128,256]{1,0:T(8,128)(2,1)} %param.9) | copy-start | bytes 196612
  6.5 83.9 %all-gather.2.cloned.1.call-start = ((), (), s32[]{:S(2)}) async-start(), calls=%async_computation | async-start | bytes 8650752 | tf_op jit(solution)/shard_map/all_gather | solution.py:14
  104.0 26.7 %copy-start.2 = (f32[256]{0:T(256)S(1)}, f32[256]{0:T(256)}, u32[]{:S(2)}) copy-start(f32[256]{0:T(256)} %param.10) | copy-start | bytes 3076
  130.8 23.3 %copy-start.3 = (f32[256]{0:T(256)S(1)}, f32[256]{0:T(256)}, u32[]{:S(2)}) copy-start(f32[256]{0:T(256)} %param.11) | copy-start | bytes 3076
  130.8 24.5 %copy-start.1 = (bf16[128,256]{1,0:T(8,128)(2,1)S(1)}, bf16[128,256]{1,0:T(8,128)(2,1)}, u32[]{:S(2)}) copy-start(bf16[128,256]{1,0:T(8,128)(2,1)} %param.9) | copy-start | bytes 196612
Sparse Core Ops, SparseCore 0:
  10.2 80.1 all-gather.1
where the time goes:
time: 162 us
  waiting for transfers between devices  82 us (51%)
  matrix products  36.5 us (23%)
  local copies, waits for them, and re-layouts  26.8 us (17%)
  between operations  13.5 us (8%)
  other arithmetic  3.36 us (2%)
    all_gather x1, waiting for transfers between devices, per_device(): gathered = lax.all_gather(features, 'rows', axis=0, tiled=True)  81.3 us
    gather x1, local copies, waits for them, and re-layouts, per_device(): picked_rows = panel_blocks[positions]  26.7 us
    dot_general x1, matrix products, per_device(): jnp.einsum('bkij,bkjh->bih', tile_block, picked_rows, preferred_element_t...  22.8 us
    dot_general x1, matrix products, per_device(): jnp.dot(gathered, weight, preferred_element_type=jnp.float32)  13.6 us
  transfers between devices with their start and end apart: 1, of which 1 were waited for; matrix products, arithmetic and copies ran while one was open for 1% of the time, Pallas kernels for 0%

commit v1 on v0

v1 whole, which is shorter than its diff:
```python
import functools

import jax
import jax.numpy as jnp
from jax import lax
from jax.experimental import pallas as pl
from jax.experimental.pallas import tpu as pltpu
from jax.sharding import PartitionSpec as P

MESH = pl.DeviceIdType.MESH

ORDERS = ("xzy", "yzx", "zxy", "zyx")


def normed(hidden, gain):
    row_mean = jnp.mean(hidden, axis=1, keepdims=True)
    centered = hidden - row_mean
    row_var = jnp.mean(centered * centered, axis=1, keepdims=True)
    return (centered / jnp.sqrt(row_var + 1e-05) * gain).astype(jnp.bfloat16)


def kernel(
    rows, fuse_norm, feat, weight, bias, gain, lookup, tiles, out,
    panel, held, acc, send_sem, recv_sem, own_sem, tile_sem,
):
    depth_z = rows // 8
    steps = depth_z * 4
    shard_rows = feat.shape[0]
    piece_rows = shard_rows // len(ORDERS)
    row_blocks, slots, block = tiles.shape[0], tiles.shape[1], tiles.shape[2]
    shard_blocks = shard_rows // block

    me = lax.axis_index("rows")
    core = me % 2
    x = (me // 2) % 2
    y = (me // 4) % 2
    z = me // 8
    x_peer = me + 2 - 4 * x
    y_peer = me + 4 - 8 * y
    core_peer = me + 1 - 2 * core
    up, down = me + 8, me - 8
    has_up, has_down = z < depth_z - 1, z > 0

    own = pltpu.make_async_copy(feat, panel.at[me], own_sem)
    own.start()

    barrier = pltpu.get_barrier_semaphore()
    for peer in (x_peer, y_peer, core_peer):
        pl.semaphore_signal(barrier, inc=1, device_id={"rows": peer}, device_id_type=MESH)

    @pl.when(has_up)
    def _():
        pl.semaphore_signal(barrier, inc=1, device_id={"rows": up}, device_id_type=MESH)

    @pl.when(has_down)
    def _():
        pl.semaphore_signal(barrier, inc=1, device_id={"rows": down}, device_id_type=MESH)

    pl.semaphore_wait(barrier, 3 + jnp.where(has_up, 1, 0) + jnp.where(has_down, 1, 0))

    def source(s):
        j, ey, ex = s // 4, (s // 2) % 2, s % 2
        low = z < depth_z - 1 - z
        near = jnp.where(low, z, depth_z - 1 - z)
        far_way = jnp.where(low, 1, -1)
        both = j <= 2 * near
        distance = jnp.where(both, (j + 1) // 2, j - near)
        way = jnp.where(jnp.logical_and(both, j % 2 == 1), -far_way, far_way)
        zs = z + way * distance
        ys, xs = (y + ey) % 2, (x + ex) % 2
        chip = (zs * 2 + ys) * 2 + xs
        return chip, zs, ey, ex

    def piece(cls, origin):
        return panel.at[origin, pl.ds(cls * piece_rows, piece_rows)]

    def copy(cls, origin, way, s, peer):
        return pltpu.make_async_remote_copy(
            src_ref=piece(cls, origin),
            dst_ref=piece(cls, origin),
            send_sem=send_sem.at[cls, way, s],
            recv_sem=recv_sem.at[cls, origin],
            device_id={"rows": peer},
            device_id_type=MESH,
        )

    def sends(cls, s, act):
        chip, zs, ey, ex = source(s)
        origin = chip * 2 + core
        still = {"x": ex == 0, "y": ey == 0, "z": zs == z}
        order = ORDERS[cls]

        def clear(axis):
            later = [still[a] for a in order[order.index(axis) + 1:]]
            return functools.reduce(jnp.logical_and, later, s >= 0)

        plan = (
            (0, up, clear("z") & has_up & (zs <= z)),
            (1, down, clear("z") & has_down & (zs >= z)),
            (2, x_peer, clear("x") & still["x"]),
            (3, y_peer, clear("y") & still["y"]),
        )
        for way, peer, cond in plan:
            pl.when(cond)(functools.partial(act, cls, origin, way, s, peer))
        act(cls, origin, 4, s, core_peer)

    def start(*what):
        copy(*what).start()

    def finish(*what):
        copy(*what).wait_send()

    acc[...] = jnp.zeros_like(acc)
    for b in range(row_blocks):
        held[b, slots] = jnp.zeros(held.shape[2:], held.dtype)
    own.wait()

    tile_copies = [
        pltpu.make_async_copy(tiles.at[b], held.at[b, pl.ds(0, slots)], tile_sem.at[b])
        for b in range(row_blocks)
    ]

    def multiply(q, carry):
        chip = source(q // 2)[0]
        origin = chip * 2 + (core + q) % 2

        @pl.when(q % 2 == 1)
        def _():
            for cls in range(len(ORDERS)):
                copy(cls, origin, 4, 0, core_peer).wait_recv()

        first = origin * shard_blocks
        left = jnp.concatenate(
            [
                jnp.concatenate(
                    [held[b, lookup[b, first + c]] for c in range(shard_blocks)], axis=1
                )
                for b in range(row_blocks)
            ],
            axis=0,
        )
        acc[...] += jnp.dot(left, panel[origin], preferred_element_type=jnp.float32)
        return carry

    def done_after(s):
        return jnp.maximum(0, jnp.minimum(2 * s + 1, 4 * s - 8))

    def step(s, carry):
        @pl.when(s < steps)
        def _():
            origin = source(s)[0] * 2 + core
            for cls in range(len(ORDERS)):
                @pl.when(s > 0)
                def _():
                    copy(cls, origin, 4, 0, core_peer).wait_recv()

                sends(cls, s, start)

        @pl.when(s == 0)
        def _():
            for c in tile_copies:
                c.start()

        @pl.when(s == 3)
        def _():
            for c in tile_copies:
                c.wait()

        lax.fori_loop(done_after(s - 1), jnp.minimum(done_after(s), 2 * steps), multiply, 0)
        return carry

    lax.fori_loop(0, steps + 1, step, 0)

    w = weight[...]
    for b in range(row_blocks):
        part = pl.ds(b * block, block)
        total = acc[part]
        high = total.astype(jnp.bfloat16)
        rest = (total - high.astype(jnp.float32)).astype(jnp.bfloat16)
        summed = jnp.dot(high, w, preferred_element_type=jnp.float32)
        summed += jnp.dot(rest, w, preferred_element_type=jnp.float32)
        if fuse_norm:
            out[part] = normed(jnp.maximum(summed + bias[...], 0.0), gain[...])
        else:
            out[part] = summed

    def drain(s, carry):
        for cls in range(len(ORDERS)):
            sends(cls, s, finish)
        return carry

    lax.fori_loop(0, steps, drain, 0)


def per_device(
    rows, reps, features, weight, shift_bias, norm_gain, tile_values, tile_cols, tile_counts, block_order
):
    row_blocks, _, slots, block, _ = tile_values.shape
    shard_rows, width = features.shape
    hidden_width = weight.shape[1]
    set_blocks = rows * shard_rows // block
    order = lax.dynamic_index_in_dim(block_order, lax.axis_index("rep"), 0, keepdims=False)
    numbers = jnp.arange(set_blocks, dtype=jnp.int32)
    number_at = jnp.sum(jnp.where(order[:, None] == numbers[None, :], numbers[:, None], 0), axis=0)
    ids = tile_cols.reshape(row_blocks, slots)
    slot = jnp.arange(slots, dtype=jnp.int32)[None, :]
    ids = jnp.where(slot < tile_counts.reshape(row_blocks, 1), ids, -1)
    hit = ids[:, :, None] == number_at[None, None, :]
    lookup = slots + jnp.sum(jnp.where(hit, slot[:, :, None] - slots, 0), axis=1)

    fuse_norm = reps == 1
    nodes = row_blocks * block
    vmem = pl.BlockSpec(memory_space=pltpu.VMEM)
    hbm = pl.BlockSpec(memory_space=pl.ANY)
    summed = pl.pallas_call(
        functools.partial(kernel, rows, fuse_norm),
        out_shape=jax.ShapeDtypeStruct(
            (nodes, hidden_width), jnp.bfloat16 if fuse_norm else jnp.float32
        ),
        in_specs=[hbm, vmem, vmem, vmem, pl.BlockSpec(memory_space=pltpu.SMEM), hbm],
        out_specs=vmem,
        scratch_shapes=[
            pltpu.VMEM((rows, shard_rows, width), jnp.bfloat16),
            pltpu.VMEM((row_blocks, slots + 1, block, block), jnp.bfloat16),
            pltpu.VMEM((nodes, width), jnp.float32),
            pltpu.SemaphoreType.DMA((len(ORDERS), 5, rows // 2)),
            pltpu.SemaphoreType.DMA((len(ORDERS), rows)),
            pltpu.SemaphoreType.DMA,
            pltpu.SemaphoreType.DMA((row_blocks,)),
        ],
        compiler_params=pltpu.CompilerParams(
            collective_id=0, has_side_effects=True, vmem_limit_bytes=52 * 1024 * 1024
        ),
    )(
        features, weight, shift_bias[None, :], norm_gain[None, :], lookup,
        tile_values.reshape(row_blocks, slots, block, block),
    )
    if fuse_norm:
        return summed
    mine = lax.psum_scatter(summed, "rep", scatter_dimension=0, tiled=True)
    return normed(jnp.maximum(mine + shift_bias, 0.0), norm_gain)


def solution(mesh):
    in_specs = (
        P(("rows", "rep"), None),
        P(),
        P(),
        P(),
        P("rows", "rep", None, None, None),
        P("rows", "rep", None),
        P("rows", "rep"),
        P(),
    )
    out_specs = P(("rows", "rep"), None)
    return jax.shard_map(
        functools.partial(per_device, mesh.shape["rows"], mesh.shape["rep"]),
        mesh=mesh, in_specs=in_specs, out_specs=out_specs, check_vma=False,
    )
```

time: 162 us -> 73.7 us (0.45)
  waiting for transfers between devices: 82 us -> 0 us
  Pallas kernels: 0 us -> 67.7 us
  matrix products: 36.5 us -> 0 us
  local copies, waits for them, and re-layouts: 26.8 us -> 3.94 us
  between operations: 13.5 us -> 0.04 us
    all_gather x1 -> x0, waiting for transfers between devices: 81.3 us -> none  [per_device(): gathered = lax.all_gather(features, 'rows', axis=0, tiled=True)]
    pallas_call x0 -> x1, Pallas kernels: none -> 67.7 us  [per_device(): pl.pallas_call(functools.partial(kernel, rows, fuse_norm), out_shape=jax....]
    dot_general x2 -> x0, matrix products: 36.5 us -> none  [the longest x1 22.8 us: per_device(): jnp.einsum('bkij,bkjh->bih', tile_block, picked_rows, preferred_element_t...]
    gather x1 -> x0, local copies, waits for them, and re-layouts: 26.7 us -> none  [per_device(): picked_rows = panel_blocks[positions]]
    unnamed x8 -> x9, local copies, waits for them, and re-layouts: 0.02 us -> 3.94 us
  transfers between devices with their start and end apart: 1 -> 0, of which waited for: 1 -> 0; matrix products, arithmetic and copies ran while one was open for 1% -> 0% of each run, Pallas kernels for 0% -> 0%
where the time goes in v1:
time: 73.7 us; the launch traced here: 73.4 us
  Pallas kernels  67.7 us (92%)
  local copies, waits for them, and re-layouts  3.94 us (5%)
  other arithmetic  1.75 us (2%)
    pallas_call x1, Pallas kernels, per_device(): pl.pallas_call(functools.partial(kernel, rows, fuse_norm), out_shape=jax....  67.7 us
    unnamed x9, local copies, waits for them, and re-layouts  3.94 us

profile of v1, /device:TPU:0, one launch (start us, length us, event | category | flops | bytes accessed | tf_op | source)
XLA Modules:
  0.0 73.4 jit_solution(3559930759893997243)
XLA Ops:
  0.0 0.8 %select_reduce_fusion.1 = s32[256]{0:T(256)S(1)} fusion(s32[256]{0:T(256)} %bitcast.10), kind=kLoop, calls=%fused_computation.1 | loop fusion | flops 196352 | bytes 2048 | tf_op jit(solution)/shard_map/reduce_sum | solution.py:204
  0.8 0.8 %fusion = s32[8,88]{1,0:T(8,128)S(1)} fusion(s32[8,88]{1,0:T(8,128)} %bitcast.9, s32[8]{0:T(128)} %bitcast.11), kind=kLoop, calls=%fused_computation.5 | loop fusion | flops 1408 | bytes 5664 | tf_op jit(solution)/shard_map/jit(_where)/select_n | solution.py:207
  1.6 0.2 select_reduce_fusion
  1.8 0.0 copy-start
  1.8 0.9 %copy-done = bf16[1024,128]{1,0:T(8,128)(2,1)S(1)} copy-done((bf16[1024,128]{1,0:T(8,128)(2,1)S(1)}, bf16[1024,128]{1,0:T(8,128)(2,1)}, u32[]{:S(2)}) %copy-start) | copy-done | bytes 262168
  2.7 0.0 copy-start.1
  2.7 0.8 %copy-done.1 = bf16[128,256]{1,0:T(8,128)(2,1)S(1)} copy-done((bf16[128,256]{1,0:T(8,128)(2,1)S(1)}, bf16[128,256]{1,0:T(8,128)(2,1)}, u32[]{:S(2)}) %copy-start.1) | copy-done | bytes 65560
  3.6 0.0 copy-start.2
  3.6 0.7 copy-done.2
  4.2 0.0 copy-start.3
  4.2 0.7 copy-done.3
  4.9 67.7 %shard_map.85 = bf16[1024,256]{1,0:T(8,128)(2,1)S(1)} custom-call(bf16[1024,128]{1,0:T(8,128)(2,1)S(1)} %copy-done, bf16[128,256]{1,0:T(8,128)(2,1)S(1)} %copy-done.1, f32[1,256]{1,0:T(1,128)S(1)} %bitcast.6, f32[1,256]{1,0:T(1,128)S(1)} %bitcast.7, s32[8,256]{1,0:T(8,128)S(1)} %broadcast_add_fusion.lookup, bf16[8,88,128,128]{3,2,1,0:T(8,128)(2,1)} %bitcast.8), custom_call_target="tpu_custom_call" | custom-call | tf_op jit(solution)/shard_map/pallas_call | solution.py:215
  72.6 0.8 %copy.10 = bf16[1024,256]{1,0:T(8,128)(2,1)} copy(bf16[1024,256]{1,0:T(8,128)(2,1)S(1)} %shard_map.85) | data formatting | bytes 1048576
  (2 shorter events, 0.0 us)
Async XLA Ops:
  1.8 1.0 %copy-start = (bf16[1024,128]{1,0:T(8,128)(2,1)S(1)}, bf16[1024,128]{1,0:T(8,128)(2,1)}, u32[]{:S(2)}) copy-start(bf16[1024,128]{1,0:T(8,128)(2,1)} %feat.1) | copy-start | bytes 786436
  2.7 0.8 %copy-start.1 = (bf16[128,256]{1,0:T(8,128)(2,1)S(1)}, bf16[128,256]{1,0:T(8,128)(2,1)}, u32[]{:S(2)}) copy-start(bf16[128,256]{1,0:T(8,128)(2,1)} %weight.1) | copy-start | bytes 196612
  3.6 0.7 copy-start.2
  4.2 0.7 copy-start.3

commit v2 on v1

v2 whole, which is shorter than its diff:
```python
import functools
import heapq

import jax
import jax.numpy as jnp
from jax import lax
from jax.experimental import pallas as pl
from jax.experimental.pallas import tpu as pltpu
from jax.sharding import PartitionSpec as P

MESH = pl.DeviceIdType.MESH

ORDERS = ("xzy", "yzx", "zxy", "zyx")


def normed(hidden, gain):
    row_mean = jnp.mean(hidden, axis=1, keepdims=True)
    centered = hidden - row_mean
    row_var = jnp.mean(centered * centered, axis=1, keepdims=True)
    return (centered / jnp.sqrt(row_var + 1e-05) * gain).astype(jnp.bfloat16)


def visit(depth, z, s, choose):
    j = s // 4
    low = z < depth - 1 - z
    near = choose(low, z, depth - 1 - z)
    far_way = choose(low, 1, -1)
    both = j <= 2 * near
    distance = choose(both, (j + 1) // 2, j - near)
    way = choose(both & (j % 2 == 1), -far_way, far_way)
    return z + way * distance


def arrivals(depth, program):
    chips = [(z, y, x) for z in range(depth) for y in range(2) for x in range(2)]
    events = [(0.0, k, chip, None) for k, chip in enumerate(chips)]
    count, free, seen, at = len(events), {}, {}, dict.fromkeys(chips, 0)

    def forward(chip, cls, origin, now):
        nonlocal count
        order = ORDERS[cls]
        for axis, step in (("z", 1), ("z", -1), ("y", 0), ("x", 0)):
            k = "zyx".index(axis)
            if any(chip["zyx".index(a)] != origin["zyx".index(a)] for a in order[order.index(axis) + 1:]):
                continue
            if axis == "z":
                target = chip[0] + step
                if not 0 <= target < depth or (chip[0] - origin[0]) * step < 0:
                    continue
            elif chip[k] != origin[k]:
                continue
            else:
                target = 1 - chip[k]
            peer = chip[:k] + (target,) + chip[k + 1:]
            end = max(free.get((chip, peer), 0.0), now) + 1.0
            free[chip, peer] = end
            heapq.heappush(events, (end + 0.55, count, peer, (cls, origin)))
            count += 1

    while events:
        now, _, chip, item = heapq.heappop(events)
        if item is not None:
            seen[(chip,) + item] = now
        if program is None:
            for cls, origin in [item] if item else [(c, chip) for c in range(len(ORDERS))]:
                forward(chip, cls, origin, now)
            continue
        while at[chip] < len(program):
            cls, s = program[at[chip]]
            z, y, x = chip
            origin = (visit(depth, z, s, lambda c, a, b: a if c else b), (y + s // 2) % 2, (x + s) % 2)
            if s > 0 and (chip, cls, origin) not in seen:
                break
            forward(chip, cls, origin, now)
            at[chip] += 1
    return chips, seen


def make_program(depth):
    program = None
    for _ in range(2):
        chips, seen = arrivals(depth, program)
        total = {}
        for z, y, x in chips:
            for cls in range(len(ORDERS)):
                for s in range(1, 4 * depth):
                    origin = (visit(depth, z, s, lambda c, a, b: a if c else b), (y + s // 2) % 2, (x + s) % 2)
                    total[cls, s] = total.get((cls, s), 0.0) + seen[(z, y, x), cls, origin]
        program = [(cls, 0) for cls in range(len(ORDERS))]
        program += sorted(total, key=lambda item: (round(total[item], 6), item))
    return program


def kernel(
    rows, program, fuse_norm, feat, weight_hbm, bias_hbm, gain_hbm, lookup_hbm, tiles, out,
    panel, held, acc, weight, bias, gain, lookup, send_sem, recv_sem, own_sem, tile_sem, small_sem,
):
    depth_z = rows // 8
    steps = depth_z * 4
    items = len(program)
    shard_rows, width = feat.shape
    piece_rows = shard_rows // len(ORDERS)
    row_blocks, slots, block = tiles.shape[0], tiles.shape[1], tiles.shape[2]
    shard_blocks = shard_rows // block
    piece_blocks = piece_rows // block

    me = lax.axis_index("rows")
    core = me % 2
    x = (me // 2) % 2
    y = (me // 4) % 2
    z = me // 8
    x_peer = me + 2 - 4 * x
    y_peer = me + 4 - 8 * y
    core_peer = me + 1 - 2 * core
    up, down = me + 8, me - 8
    has_up, has_down = z < depth_z - 1, z > 0

    own = pltpu.make_async_copy(feat, panel.at[me], own_sem)
    own.start()

    barrier = pltpu.get_barrier_semaphore()
    for peer in (x_peer, y_peer, core_peer):
        pl.semaphore_signal(barrier, inc=1, device_id={"rows": peer}, device_id_type=MESH)

    @pl.when(has_up)
    def _():
        pl.semaphore_signal(barrier, inc=1, device_id={"rows": up}, device_id_type=MESH)

    @pl.when(has_down)
    def _():
        pl.semaphore_signal(barrier, inc=1, device_id={"rows": down}, device_id_type=MESH)

    small_copies = [
        pltpu.make_async_copy(there, here, small_sem.at[k])
        for k, (there, here) in enumerate(
            ((lookup_hbm, lookup), (weight_hbm, weight), (bias_hbm, bias), (gain_hbm, gain))
        )
    ]
    tile_copies = [
        pltpu.make_async_copy(tiles.at[b], held.at[b, pl.ds(0, slots)], tile_sem.at[b])
        for b in range(row_blocks)
    ]
    for c in small_copies + tile_copies:
        c.start()
    own.wait()
    pl.semaphore_wait(barrier, 3 + jnp.where(has_up, 1, 0) + jnp.where(has_down, 1, 0))

    def chip_of(s):
        zs = visit(depth_z, z, s, jnp.where)
        return (zs * 2 + (y + s // 2) % 2) * 2 + (x + s) % 2, zs

    def copy(cls, origin, sem, peer):
        piece = panel.at[origin, pl.ds(cls * piece_rows, piece_rows)]
        return pltpu.make_async_remote_copy(
            src_ref=piece,
            dst_ref=piece,
            send_sem=send_sem.at[sem],
            recv_sem=recv_sem.at[cls, origin],
            device_id={"rows": peer},
            device_id_type=MESH,
        )

    numbers = {}

    def take(cls, s, act):
        chip, zs = chip_of(s)
        origin = chip * 2 + core
        order = ORDERS[cls]
        still = {"x": s % 2 == 0, "y": (s // 2) % 2 == 0, "z": s < 4}

        def send(name, peer, cond=None):
            sem = numbers.setdefault((cls, s, name), len(numbers))
            if cond is None:
                act(cls, origin, sem, peer)
            else:
                pl.when(cond)(functools.partial(act, cls, origin, sem, peer))

        def clear(axis):
            return all(still[a] for a in order[order.index(axis) + 1:])

        if clear("z"):
            if still["z"]:
                send("up", up, has_up)
                send("down", down, has_down)
            else:
                send("up", up, has_up & (zs < z))
                send("down", down, has_down & (zs > z))
        if clear("y") and still["y"]:
            send("y", y_peer)
        if clear("x") and still["x"]:
            send("x", x_peer)
        send("core", core_peer)

    def start(*what):
        copy(*what).start()

    def finish(*what):
        copy(*what).wait_send()

    def item_step(k):
        cls, s = program[k]
        if s > 0:
            copy(cls, chip_of(s)[0] * 2 + core, 0, core_peer).wait_recv()
        take(cls, s, start)

    def dispatch(i, low, high):
        if high - low == 1:
            item_step(low)
            return
        middle = (low + high) // 2
        pl.when(i < middle)(lambda: dispatch(i, low, middle))
        pl.when(i >= middle)(lambda: dispatch(i, middle, high))

    bits = (items - 1).bit_length()
    per_word = 30 // bits
    words = [
        sum((cls * steps + s) << (bits * k) for k, (cls, s) in enumerate(program[w:w + per_word]))
        for w in range(0, items, per_word)
    ]

    def entry(q):
        which = q // per_word
        word = jnp.int32(words[0])
        for k in range(1, len(words)):
            word = jnp.where(which == k, words[k], word)
        code = lax.shift_right_logical(word, (q - which * per_word) * bits) & (2**bits - 1)
        return code // steps, code % steps

    def multiply(q, carry):
        cls, s = entry(q)
        chip = chip_of(s)[0]
        copy(cls, chip * 2 + 1 - core, 0, core_peer).wait_recv()
        right = panel[pl.ds(chip * 2, 2), pl.ds(pl.multiple_of(cls * piece_rows, piece_rows), piece_rows)]
        right = right.reshape(2 * piece_rows, width)
        columns = [
            (chip * 2 + c) * shard_blocks + cls * piece_blocks + k
            for c in range(2) for k in range(piece_blocks)
        ]
        left = jnp.concatenate(
            [
                jnp.concatenate([held[b, lookup[b, c]] for c in columns], axis=1)
                for b in range(row_blocks)
            ],
            axis=0,
        )
        acc[...] += jnp.dot(left, right, preferred_element_type=jnp.float32)
        return carry

    acc[...] = jnp.zeros_like(acc)
    for b in range(row_blocks):
        held[b, slots] = jnp.zeros(held.shape[2:], held.dtype)

    begin = items * 3 // 16

    def done_after(i):
        return jnp.maximum(0, jnp.minimum(i, (i - begin) * 3 // 2))

    def step(i, carry):
        pl.when(i < items)(lambda: dispatch(i, 0, items))

        @pl.when(i == begin)
        def _():
            for c in small_copies + tile_copies:
                c.wait()

        lax.fori_loop(done_after(i - 1), done_after(i), multiply, 0)
        return carry

    lax.fori_loop(0, items + 1, step, 0)

    w = weight[...]
    for b in range(row_blocks):
        part = pl.ds(b * block, block)
        total = acc[part]
        high = total.astype(jnp.bfloat16)
        rest = (total - high.astype(jnp.float32)).astype(jnp.bfloat16)
        summed = jnp.dot(high, w, preferred_element_type=jnp.float32)
        summed += jnp.dot(rest, w, preferred_element_type=jnp.float32)
        if fuse_norm:
            out[part] = normed(jnp.maximum(summed + bias[...], 0.0), gain[...])
        else:
            out[part] = summed

    for cls, s in program:
        take(cls, s, finish)


def per_device(
    rows, reps, program, features, weight, shift_bias, norm_gain, tile_values, tile_cols, tile_counts, block_order
):
    row_blocks, _, slots, block, _ = tile_values.shape
    shard_rows, width = features.shape
    hidden_width = weight.shape[1]
    set_blocks = rows * shard_rows // block
    order = lax.dynamic_index_in_dim(block_order, lax.axis_index("rep"), 0, keepdims=False)
    numbers = jnp.arange(set_blocks, dtype=jnp.int32)
    number_at = jnp.sum(jnp.where(order[:, None] == numbers[None, :], numbers[:, None], 0), axis=0)
    ids = tile_cols.reshape(row_blocks, slots)
    slot = jnp.arange(slots, dtype=jnp.int32)[None, :]
    ids = jnp.where(slot < tile_counts.reshape(row_blocks, 1), ids, -1)
    hit = ids[:, :, None] == number_at[None, None, :]
    lookup = slots + jnp.sum(jnp.where(hit, slot[:, :, None] - slots, 0), axis=1)

    fuse_norm = reps == 1
    nodes = row_blocks * block
    vmem = pl.BlockSpec(memory_space=pltpu.VMEM)
    hbm = pl.BlockSpec(memory_space=pl.ANY)
    summed = pl.pallas_call(
        functools.partial(kernel, rows, program, fuse_norm),
        out_shape=jax.ShapeDtypeStruct(
            (nodes, hidden_width), jnp.bfloat16 if fuse_norm else jnp.float32
        ),
        in_specs=[hbm] * 6,
        out_specs=vmem,
        scratch_shapes=[
            pltpu.VMEM((rows, shard_rows, width), jnp.bfloat16),
            pltpu.VMEM((row_blocks, slots + 1, block, block), jnp.bfloat16),
            pltpu.VMEM((nodes, width), jnp.float32),
            pltpu.VMEM(weight.shape, weight.dtype),
            pltpu.VMEM((1, hidden_width), jnp.float32),
            pltpu.VMEM((1, hidden_width), jnp.float32),
            pltpu.SMEM(lookup.shape, jnp.int32),
            pltpu.SemaphoreType.DMA((5 * len(program),)),
            pltpu.SemaphoreType.DMA((len(ORDERS), rows)),
            pltpu.SemaphoreType.DMA,
            pltpu.SemaphoreType.DMA((row_blocks,)),
            pltpu.SemaphoreType.DMA((4,)),
        ],
        compiler_params=pltpu.CompilerParams(
            collective_id=0, has_side_effects=True, vmem_limit_bytes=52 * 1024 * 1024
        ),
    )(
        features, weight, shift_bias[None, :], norm_gain[None, :], lookup,
        tile_values.reshape(row_blocks, slots, block, block),
    )
    if fuse_norm:
        return summed
    mine = lax.psum_scatter(summed, "rep", scatter_dimension=0, tiled=True)
    return normed(jnp.maximum(mine + shift_bias, 0.0), norm_gain)


def solution(mesh):
    program = make_program(mesh.shape["rows"] // 8)
    in_specs = (
        P(("rows", "rep"), None),
        P(),
        P(),
        P(),
        P("rows", "rep", None, None, None),
        P("rows", "rep", None),
        P("rows", "rep"),
        P(),
    )
    out_specs = P(("rows", "rep"), None)
    return jax.shard_map(
        functools.partial(per_device, mesh.shape["rows"], mesh.shape["rep"], program),
        mesh=mesh, in_specs=in_specs, out_specs=out_specs, check_vma=False,
    )
```

time: 73.7 us -> 67.1 us (0.910)
  Pallas kernels: 67.7 us -> 61.1 us
    pallas_call x1, Pallas kernels: 67.7 us -> 61.1 us  [per_device(): pl.pallas_call(functools.partial(kernel, rows, program, fuse_norm), out_s...]
where the time goes in v2:
time: 67.1 us; the launch traced here: 66.8 us
  Pallas kernels  61.1 us (91%)
  local copies, waits for them, and re-layouts  3.94 us (6%)
  other arithmetic  1.75 us (3%)
    pallas_call x1, Pallas kernels, per_device(): pl.pallas_call(functools.partial(kernel, rows, program, fuse_norm), out_s...  61.1 us
    unnamed x9, local copies, waits for them, and re-layouts  3.94 us

profile of v2, /device:TPU:0, one launch (start us, length us, event | category | flops | bytes accessed | tf_op | source)
XLA Modules:
  0.0 66.8 jit_solution(4518918131445430967)
XLA Ops:
  0.0 0.8 %select_reduce_fusion.1 = s32[256]{0:T(256)S(1)} fusion(s32[256]{0:T(256)} %bitcast.10), kind=kLoop, calls=%fused_computation.1 | loop fusion | flops 196352 | bytes 2048 | tf_op jit(solution)/shard_map/reduce_sum | solution.py:297
  0.8 0.8 %fusion = s32[8,88]{1,0:T(8,128)S(1)} fusion(s32[8,88]{1,0:T(8,128)} %bitcast.9, s32[8]{0:T(128)} %bitcast.11), kind=kLoop, calls=%fused_computation.5 | loop fusion | flops 1408 | bytes 5664 | tf_op jit(solution)/shard_map/jit(_where)/select_n | solution.py:300
  1.6 0.2 select_reduce_fusion
  1.8 0.0 copy-start
  1.8 0.9 %copy-done = bf16[1024,128]{1,0:T(8,128)(2,1)S(1)} copy-done((bf16[1024,128]{1,0:T(8,128)(2,1)S(1)}, bf16[1024,128]{1,0:T(8,128)(2,1)}, u32[]{:S(2)}) %copy-start) | copy-done | bytes 262168
  2.7 0.0 copy-start.1
  2.7 0.8 %copy-done.1 = bf16[128,256]{1,0:T(8,128)(2,1)S(1)} copy-done((bf16[128,256]{1,0:T(8,128)(2,1)S(1)}, bf16[128,256]{1,0:T(8,128)(2,1)}, u32[]{:S(2)}) %copy-start.1) | copy-done | bytes 65560
  3.6 0.0 copy-start.2
  3.6 0.7 %copy-done.2 = f32[256]{0:T(256)S(1)} copy-done((f32[256]{0:T(256)S(1)}, f32[256]{0:T(256)}, u32[]{:S(2)}) %copy-start.2) | copy-done | bytes 1048
  4.2 0.0 copy-start.3
  4.2 0.7 %copy-done.3 = f32[256]{0:T(256)S(1)} copy-done((f32[256]{0:T(256)S(1)}, f32[256]{0:T(256)}, u32[]{:S(2)}) %copy-start.3) | copy-done | bytes 1048
  4.9 61.1 %shard_map.85 = bf16[1024,256]{1,0:T(8,128)(2,1)S(1)} custom-call(bf16[1024,128]{1,0:T(8,128)(2,1)S(1)} %copy-done, bf16[128,256]{1,0:T(8,128)(2,1)S(1)} %copy-done.1, f32[1,256]{1,0:T(1,128)S(1)} %bitcast.6, f32[1,256]{1,0:T(1,128)S(1)} %bitcast.7, s32[8,256]{1,0:T(8,128)S(1)} %broadcast_add_fusion.lookup_hbm, bf16[8,88,128,128]{3,2,1,0:T(8,128)(2,1)} %bitcast.8), custom_call_target="tpu_custom_call" | custom-call | tf_op jit(solution)/shard_map/pallas_call | solution.py:308
  66.0 0.8 %copy.10 = bf16[1024,256]{1,0:T(8,128)(2,1)} copy(bf16[1024,256]{1,0:T(8,128)(2,1)S(1)} %shard_map.85) | data formatting | bytes 1048576
  (2 shorter events, 0.0 us)
Async XLA Ops:
  1.8 1.0 %copy-start = (bf16[1024,128]{1,0:T(8,128)(2,1)S(1)}, bf16[1024,128]{1,0:T(8,128)(2,1)}, u32[]{:S(2)}) copy-start(bf16[1024,128]{1,0:T(8,128)(2,1)} %feat.1) | copy-start | bytes 786436
  2.7 0.8 %copy-start.1 = (bf16[128,256]{1,0:T(8,128)(2,1)S(1)}, bf16[128,256]{1,0:T(8,128)(2,1)}, u32[]{:S(2)}) copy-start(bf16[128,256]{1,0:T(8,128)(2,1)} %weight_hbm.1) | copy-start | bytes 196612
  3.6 0.7 %copy-start.2 = (f32[256]{0:T(256)S(1)}, f32[256]{0:T(256)}, u32[]{:S(2)}) copy-start(f32[256]{0:T(256)} %param.10) | copy-start | bytes 3076
  4.2 0.7 %copy-start.3 = (f32[256]{0:T(256)S(1)}, f32[256]{0:T(256)}, u32[]{:S(2)}) copy-start(f32[256]{0:T(256)} %param.11) | copy-start | bytes 3076

commit v3 on v2

--- a/solution.py
+++ b/solution.py
@@ -250,10 +250,10 @@
     for b in range(row_blocks):
         held[b, slots] = jnp.zeros(held.shape[2:], held.dtype)
 
-    begin = items * 3 // 16
+    begin = items // 8
 
     def done_after(i):
-        return jnp.maximum(0, jnp.minimum(i, (i - begin) * 3 // 2))
+        return jnp.maximum(0, jnp.minimum(i, (i - begin) * 8 // 7))
 
     def step(i, carry):
         pl.when(i < items)(lambda: dispatch(i, 0, items))
@@ -327,7 +327,7 @@
             pltpu.SemaphoreType.DMA((4,)),
         ],
         compiler_params=pltpu.CompilerParams(
-            collective_id=0, has_side_effects=True, vmem_limit_bytes=52 * 1024 * 1024
+            collective_id=0, has_side_effects=True, vmem_limit_bytes=60 * 1024 * 1024
         ),
     )(
         features, weight, shift_bias[None, :], norm_gain[None, :], lookup,

time: 67.1 us -> 60.8 us (0.906)
  Pallas kernels: 61.1 us -> 56.4 us
  local copies, waits for them, and re-layouts: 3.94 us -> 1.87 us
    pallas_call x1, Pallas kernels: 61.1 us -> 56.4 us  [per_device(): pl.pallas_call(functools.partial(kernel, rows, program, fuse_norm), out_s...]
    unnamed x9 -> x1, local copies, waits for them, and re-layouts: 3.94 us -> 1.87 us
where the time goes in v3:
time: 60.8 us; the launch traced here: 60.6 us
  Pallas kernels  56.4 us (93%)
  other arithmetic  2.35 us (4%)
  local copies, waits for them, and re-layouts  1.87 us (3%)
    pallas_call x1, Pallas kernels, per_device(): pl.pallas_call(functools.partial(kernel, rows, program, fuse_norm), out_s...  56.4 us
    unnamed x1, local copies, waits for them, and re-layouts  1.87 us

profile of v3, /device:TPU:0, one launch (start us, length us, event | category | flops | bytes accessed | tf_op | source)
XLA Modules:
  0.0 60.6 jit_solution(4591825709638004898)
XLA Ops:
  0.0 0.8 %select_reduce_fusion.1 = s32[256]{0:T(256)S(1)} fusion(s32[256]{0:T(256)} %bitcast.10), kind=kLoop, calls=%fused_computation.1 | loop fusion | flops 196352 | bytes 2048 | tf_op jit(solution)/shard_map/reduce_sum | solution.py:297
  0.8 0.8 %fusion = s32[8,88]{1,0:T(8,128)S(1)} fusion(s32[8,88]{1,0:T(8,128)} %bitcast.7, s32[8]{0:T(128)} %bitcast.11), kind=kLoop, calls=%fused_computation.5 | loop fusion | flops 1408 | bytes 5664 | tf_op jit(solution)/shard_map/jit(_where)/select_n | solution.py:300
  1.6 0.2 select_reduce_fusion
  1.8 0.6 broadcast_add_fusion.lookup_hbm
  2.4 56.4 %shard_map.85 = bf16[1024,256]{1,0:T(8,128)(2,1)} custom-call(bf16[1024,128]{1,0:T(8,128)(2,1)} %feat.1, bf16[128,256]{1,0:T(8,128)(2,1)} %weight_hbm.1, f32[1,256]{1,0:T(1,128)} %bitcast.8, f32[1,256]{1,0:T(1,128)} %bitcast.9, s32[8,256]{1,0:T(8,128)} %broadcast_add_fusion.lookup_hbm, bf16[8,88,128,128]{3,2,1,0:T(8,128)(2,1)} %bitcast.6), custom_call_target="tpu_custom_call" | custom-call | tf_op jit(solution)/shard_map/pallas_call | solution.py:308
  58.8 1.9 %copy.10 = bf16[1024,256]{1,0:T(8,128)(2,1)} copy(bf16[1024,256]{1,0:T(8,128)(2,1)} %shard_map.85) | data formatting | bytes 1048576
  (1 shorter events, 0.0 us)
